TPU v7x, 32 devices: a whole 2x2x4 slice. The times are simulated.
32 devices in a mesh: blk: 16 (over z, x, core), col: 2 (over y).
Axes of the slice: x: 2, y: 2, z: 4, core: 2. Of those that a mesh axis runs over, the one named last changes fastest.
Arguments:
- feat1: bfloat16 [64, 96, 256], P('blk', 'col'), may hold values from -40 to 40
- feat2: bfloat16 [64, 96, 256], P('blk', 'col'), may hold values from -40 to 40
Outputs:
- flow: float32 [2, 64, 96], P(None, 'blk', 'col')
- grad_flow: float32 [2, 64, 96], P(None, 'blk', 'col')
- grad_warped: float32 [64, 96, 256], P('blk', 'col')
All inputs are finite; a program needn't handle non-finite values.
Results may differ from a plain program's by a relative error of at most 0.0075.
Values may be sent and summed in bfloat16 or wider, within the bound.
A program may use at most 64 MiB of HBM per device.

v0:
```python
import math

import jax
import jax.numpy as jnp
from jax import lax
from jax.sharding import PartitionSpec as P

ssim_one = 0.01
ssim_two = 0.03
charb_sq = 0.0001


def with_halo(value, sides, width):
    for axis, dim in sides:
        count, length = (lax.axis_size(axis), value.shape[dim])
        up = [(i, (i + 1) % count) for i in range(count - 1)]
        down = [(j, i) for i, j in up]
        last = lax.slice_in_dim(value, length - width, length, axis=dim)
        first = lax.slice_in_dim(value, 0, width, axis=dim)
        before = lax.ppermute(last, axis, up)
        after = lax.ppermute(first, axis, down)
        value = jnp.concatenate([before, value, after], axis=dim)
    return value


def box_valid(padded):
    rows_out = padded.shape[0] - 2
    cols_out = padded.shape[1] - 2
    total = jnp.zeros((rows_out, cols_out) + padded.shape[2:], padded.dtype)
    for offset_r in range(3):
        for offset_c in range(3):
            total = total + padded[offset_r : offset_r + rows_out, offset_c : offset_c + cols_out]
    return total / 9.0


def ssim_loss(mean_y, var_y, cov_xy, mean_x, var_x):
    top = (2.0 * mean_x * mean_y + ssim_one) * (2.0 * cov_xy + ssim_two)
    bottom = (mean_x * mean_x + mean_y * mean_y + ssim_one) * (var_x + var_y + ssim_two)
    return jnp.sum((1.0 - top / bottom) * 0.5)


def local_terms(xpad, ypad):
    mean_x = box_valid(xpad)
    mean_y = box_valid(ypad)
    var_x = box_valid(xpad * xpad) - mean_x * mean_x
    var_y = box_valid(ypad * ypad) - mean_y * mean_y
    cov_xy = box_valid(xpad * ypad) - mean_x * mean_y
    loss, pull = jax.vjp(
        lambda one, two, three: ssim_loss(one, two, three, mean_x, var_x), mean_y, var_y, cov_xy
    )
    grad_mean, grad_var, grad_cov = pull(jnp.ones_like(loss))
    first = grad_mean - 2.0 * grad_var * mean_y - grad_cov * mean_x
    return (first, grad_var, grad_cov)


def edge_weight(lower, upper):
    return jnp.exp(-jnp.mean(jnp.abs(upper - lower), axis=-1))


def charbonnier(weight, delta):
    return weight * delta / jnp.sqrt(delta * delta + charb_sq)


def absorb(carry, queries, keys, key_y, key_x, scale):
    total_keys = keys.shape[0]
    width = keys.shape[1]
    step = min(total_keys, 2048)
    while total_keys % step != 0:
        step = step - 1
    blocks = total_keys // step

    def visit(state, item):
        top, total, acc, along_y, along_x = state
        key_block, block_y, block_x = item
        score = (
            lax.dot_general(
                queries, key_block, (((1,), (1,)), ((), ())), preferred_element_type=jnp.float32
            )
            * scale
        )
        new_top = jnp.maximum(top, jnp.max(score, axis=1))
        shrink = jnp.exp(top - new_top)
        expo = jnp.exp(score - new_top[:, None])
        total = total * shrink + jnp.sum(expo, axis=1)
        acc = acc * shrink[:, None] + jnp.dot(
            expo.astype(jnp.bfloat16), key_block, preferred_element_type=jnp.float32
        )
        along_y = along_y * shrink + jnp.sum(expo * block_y[None, :], axis=1)
        along_x = along_x * shrink + jnp.sum(expo * block_x[None, :], axis=1)
        return ((new_top, total, acc, along_y, along_x), None)

    items = (
        keys.reshape(blocks, step, width),
        key_y.reshape(blocks, step),
        key_x.reshape(blocks, step),
    )
    carry, unused = lax.scan(visit, carry, items)
    return carry


def body(feat1, feat2):
    rows, cols, width = feat1.shape
    ncol = lax.axis_size("col")
    full_rows = rows * lax.axis_size("blk")
    full_cols = cols * ncol
    row_start = lax.axis_index("blk") * rows
    col_start = lax.axis_index("col") * cols
    scale = 1.0 / math.sqrt(width)
    tokens = rows * cols
    queries = feat1.reshape(tokens, width)
    init = (
        jnp.full((tokens,), -1e30, jnp.float32),
        jnp.zeros((tokens,), jnp.float32),
        jnp.zeros((tokens, width), jnp.float32),
        jnp.zeros((tokens,), jnp.float32),
        jnp.zeros((tokens,), jnp.float32),
    )

    def norm_y(index):
        return (index.astype(jnp.float32) + 0.5) * (2.0 / full_rows) - 1.0

    def norm_x(index):
        return (index.astype(jnp.float32) + 0.5) * (2.0 / full_cols) - 1.0

    band = lax.all_gather(feat2, "col", axis=1, tiled=True)
    piece = lax.all_gather(band, "blk", axis=0, tiled=True)
    count = piece.shape[0]
    grid_y = jnp.broadcast_to(jnp.arange(count, dtype=jnp.int32)[:, None], (count, full_cols))
    grid_x = jnp.broadcast_to(jnp.arange(full_cols, dtype=jnp.int32)[None, :], (count, full_cols))
    carry = absorb(
        init,
        queries,
        piece.reshape(count * full_cols, width),
        norm_y(grid_y).reshape(-1),
        norm_x(grid_x).reshape(-1),
        scale,
    )
    top, total, acc, along_y, along_x = carry
    warped = (acc / total[:, None]).astype(jnp.bfloat16).reshape(rows, cols, width)
    own_y = norm_y(row_start + jnp.arange(rows, dtype=jnp.int32))
    own_x = norm_x(col_start + jnp.arange(cols, dtype=jnp.int32))
    flow = jnp.stack(
        [
            (along_y / total).reshape(rows, cols) - own_y[:, None],
            (along_x / total).reshape(rows, cols) - own_x[None, :],
        ]
    )
    pair = jnp.stack([feat1, warped])
    xval = feat1.astype(jnp.float32)
    yval = warped.astype(jnp.float32)
    margin = 1
    padded = with_halo(pair, (("blk", 1), ("col", 2)), 1)
    xpad = padded[0].astype(jnp.float32)
    ypad = padded[1].astype(jnp.float32)
    first, grad_var, grad_cov = local_terms(xpad, ypad)
    maps = jnp.stack([first, grad_var, grad_cov])
    beside_all = with_halo(maps.astype(jnp.bfloat16), (("blk", 1), ("col", 2)), 1).astype(
        maps.dtype
    )
    spread_first = box_valid(beside_all[0])
    spread_var = box_valid(beside_all[1])
    spread_cov = box_valid(beside_all[2])
    grad_warped = spread_first + 2.0 * yval * spread_var + xval * spread_cov
    flow_pad = with_halo(flow, (("blk", 1), ("col", 2)), 1)
    x_rows = xpad[margin - 1 : margin + rows + 1, margin : margin + cols]
    x_cols = xpad[margin : margin + rows, margin - 1 : margin + cols + 1]
    edge_y = row_start - 1 + jnp.arange(rows + 1, dtype=jnp.int32)
    valid_y = (edge_y >= 0) & (edge_y <= full_rows - 2)
    edge_x = col_start - 1 + jnp.arange(cols + 1, dtype=jnp.int32)
    valid_x = (edge_x >= 0) & (edge_x <= full_cols - 2)
    delta_y = flow_pad[:, 1:, 1:-1] - flow_pad[:, :-1, 1:-1]
    push_y = jnp.where(
        valid_y[None, :, None],
        charbonnier(edge_weight(x_rows[:-1], x_rows[1:])[None], delta_y),
        0.0,
    )
    delta_x = flow_pad[:, 1:-1, 1:] - flow_pad[:, 1:-1, :-1]
    push_x = jnp.where(
        valid_x[None, None, :],
        charbonnier(edge_weight(x_cols[:, :-1], x_cols[:, 1:])[None], delta_x),
        0.0,
    )
    grad_flow = push_y[:, :rows] - push_y[:, 1:] + push_x[:, :, :cols] - push_x[:, :, 1:]
    return (flow, grad_flow, grad_warped)


def solution(mesh):
    placed = (P("blk", "col", None), P("blk", "col", None))
    return jax.shard_map(
        body,
        mesh=mesh,
        in_specs=placed,
        out_specs=(P(None, "blk", "col"), P(None, "blk", "col"), P("blk", "col", None)),
        check_vma=False,
    )
```

profile of v0, /device:TPU:20, one launch (start us, length us, event | category | flops | bytes accessed | tf_op | source)
XLA Modules:
  0.0 125.7 jit_solution(17241187873160933026)
XLA Ops:
  7.2 5.8 %all_gather.6 = bf16[4,96,256]{2,1,0:T(8,128)(2,1)} all-gather(bf16[4,48,256]{2,1,0:T(8,128)(2,1)} %param.5), channel_id=1, replica_groups=mesh['blk'=16,'col'=2] {'col'}, dimensions={1}, use_global_device_ids=true | all-gather | bytes 294912 | tf_op jit(solution)/shard_map/all_gather | solution.py:125
  13.5 45.7 %all-gather.2.cloned.1.call-done = bf16[64,96,256]{2,1,0:T(8,128)(2,1)} async-done(((bf16[4,96,256]{2,1,0:T(8,128)(2,1)}), bf16[64,96,256]{2,1,0:T(8,128)(2,1)}) %all-gather.2.cloned.1.call-update) | async-done | bytes 3145744 | tf_op jit(solution)/shard_map/all_gather | solution.py:126
  59.2 12.6 %while.19 = (s32[]{:T(128)}, f32[192]{0:T(256)S(1)}, f32[192]{0:T(256)S(1)}, f32[192,256]{1,0:T(8,128)S(1)}, f32[192]{0:T(256)S(1)}, /*index=5*/f32[192]{0:T(256...) while((s32[]{:T(128)}, f32[192]{0:T(256)S(1)}, ...), condition=%wide.region_5.6_spmd.clone, body=%wide.region_0.5_spmd.clone.sunk | while | flops 406734528 | bytes 7375766 | solution.py:97
  59.2 1.8 %fusion.68 = (f32[192]{0:T(256)S(1)}, f32[2048,192]{0,1:T(8,128)S(1)}) fusion(bf16[192,256]{1,0:T(8,128)(2,1)} %get-tuple-element.273, bf16[3,2048,256]{2,1,0:T(8,128)(2,1)} %get-tuple-element.272, s32[]{:T(128)S(6)} %copy.11), kind=kOutput, calls=%fused_computation.189.clone.1 | convolution fusion | flops 202112832 | bytes 2720516 | tf_op jit(solution)/shard_map/while/body/eval_jaxpr/dot_general | solution.py:76
  61.7 1.7 %convolution_add_fusion.2 = f32[192,256]{1,0:T(8,128)S(1)} fusion(bf16[3,2048,256]{2,1,0:T(8,128)(2,1)} %get-tuple-element.272, s32[]{:T(128)S(6)} %copy.11, f32[2048,192]{0,1:T(8,128)S(1)} %get-tuple-element.232, f32[192]{0:T(256)S(1)} %fusion.69, f32[192,256]{1,0:T(8,128)S(1)} %get-tuple-element.257, f32[192]{0:T(256)S(1)} %get-tuple-element.237, ...), kind=kOutput, calls=%fused_computation.4.clone.1 | convolution fusion | flops 202260480 | bytes 3016197 | tf_op jit(solution)/shard_map/while/body/eval_jaxpr/dot_general | solution.py:85
  63.4 1.8 %fusion.68 = (f32[192]{0:T(256)S(1)}, f32[2048,192]{0,1:T(8,128)S(1)}) fusion(bf16[192,256]{1,0:T(8,128)(2,1)} %get-tuple-element.273, bf16[3,2048,256]{2,1,0:T(8,128)(2,1)} %get-tuple-element.272, s32[]{:T(128)S(6)} %copy.11), kind=kOutput, calls=%fused_computation.189.clone.1 | convolution fusion | flops 202112832 | bytes 2720516 | tf_op jit(solution)/shard_map/while/body/eval_jaxpr/dot_general | solution.py:76
  65.9 1.7 %convolution_add_fusion.2 = f32[192,256]{1,0:T(8,128)S(1)} fusion(bf16[3,2048,256]{2,1,0:T(8,128)(2,1)} %get-tuple-element.272, s32[]{:T(128)S(6)} %copy.11, f32[2048,192]{0,1:T(8,128)S(1)} %get-tuple-element.232, f32[192]{0:T(256)S(1)} %fusion.69, f32[192,256]{1,0:T(8,128)S(1)} %get-tuple-element.257, f32[192]{0:T(256)S(1)} %get-tuple-element.237, ...), kind=kOutput, calls=%fused_computation.4.clone.1 | convolution fusion | flops 202260480 | bytes 3016197 | tf_op jit(solution)/shard_map/while/body/eval_jaxpr/dot_general | solution.py:85
  67.6 1.8 %fusion.68 = (f32[192]{0:T(256)S(1)}, f32[2048,192]{0,1:T(8,128)S(1)}) fusion(bf16[192,256]{1,0:T(8,128)(2,1)} %get-tuple-element.273, bf16[3,2048,256]{2,1,0:T(8,128)(2,1)} %get-tuple-element.272, s32[]{:T(128)S(6)} %copy.11), kind=kOutput, calls=%fused_computation.189.clone.1 | convolution fusion | flops 202112832 | bytes 2720516 | tf_op jit(solution)/shard_map/while/body/eval_jaxpr/dot_general | solution.py:76
  70.1 1.7 %convolution_add_fusion.2 = f32[192,256]{1,0:T(8,128)S(1)} fusion(bf16[3,2048,256]{2,1,0:T(8,128)(2,1)} %get-tuple-element.272, s32[]{:T(128)S(6)} %copy.11, f32[2048,192]{0,1:T(8,128)S(1)} %get-tuple-element.232, f32[192]{0:T(256)S(1)} %fusion.69, f32[192,256]{1,0:T(8,128)S(1)} %get-tuple-element.257, f32[192]{0:T(256)S(1)} %get-tuple-element.237, ...), kind=kOutput, calls=%fused_computation.4.clone.1 | convolution fusion | flops 202260480 | bytes 3016197 | tf_op jit(solution)/shard_map/while/body/eval_jaxpr/dot_general | solution.py:85
  72.0 3.0 %collective-permute-start.4 = (f32[2,1,48]{2,1,0:T(1,128)S(1)}, f32[2,1,48]{2,1,0:T(1,128)S(1)}, u32[]{:S(2)}, u32[]{:S(2)}) collective-permute-start(f32[2,1,48]{2,1,0:T(1,128)S(1)} %get-tuple-element.154), channel_id=1, source_target_pairs={{2,0},{4,2},{6,4},{8,6},{10,8},{12,10},{14,12},{16,14},{18,16},{20... | collective-permute-start | bytes 1160 | tf_op jit(solution)/shard_map/ppermute | solution.py:21
  75.0 1.9 %collective-permute-start.5 = (f32[2,1,48]{2,1,0:T(1,128)S(1)}, f32[2,1,48]{2,1,0:T(1,128)S(1)}, u32[]{:S(2)}, u32[]{:S(2)}) collective-permute-start(f32[2,1,48]{2,1,0:T(1,128)S(1)} %get-tuple-element.153), channel_id=1, source_target_pairs={{0,2},{2,4},{4,6},{6,8},{8,10},{10,12},{12,14},{14,16},{16,18},{18... | collective-permute-start | bytes 1160 | tf_op jit(solution)/shard_map/ppermute | solution.py:20
  78.4 4.5 %collective-permute-start.1 = (bf16[2,1,48,256]{3,2,1,0:T(8,128)(2,1)S(1)}, bf16[2,1,48,256]{3,2,1,0:T(8,128)(2,1)S(1)}, u32[]{:S(2)}, u32[]{:S(2)}) collective-permute-start(bf16[2,1,48,256]{3,2,1,0:T(8,128)(2,1)S(1)} %get-tuple-element.150), channel_id=1, source_target_pairs={{2,0},{4,2},{6,4},{8,6},{10,8},{12,10},{14,12},{16,14},{18,16},{20... | collective-permute-start | bytes 147464 | tf_op jit(solution)/shard_map/ppermute | solution.py:21
  82.9 1.9 %collective-permute-start = (bf16[2,1,48,256]{3,2,1,0:T(8,128)(2,1)S(1)}, bf16[2,1,48,256]{3,2,1,0:T(8,128)(2,1)S(1)}, u32[]{:S(2)}, u32[]{:S(2)}) collective-permute-start(bf16[2,1,48,256]{3,2,1,0:T(8,128)(2,1)S(1)} %get-tuple-element.149), channel_id=1, source_target_pairs={{0,2},{2,4},{4,6},{6,8},{8,10},{10,12},{12,14},{14,16},{16,18},{18... | collective-permute-start | bytes 147464 | tf_op jit(solution)/shard_map/ppermute | solution.py:20
  84.9 4.3 %collective-permute-done = bf16[2,1,48,256]{3,2,1,0:T(8,128)(2,1)S(1)} collective-permute-done((bf16[2,1,48,256]{3,2,1,0:T(8,128)(2,1)S(1)}, bf16[2,1,48,256]{3,2,1,0:T(8,128)(2,1)S(1)}, u32[]{:S(2)}, u32[]{:S(2)}) %collective-permute-start) | collective-permute-done | bytes 49184 | tf_op jit(solution)/shard_map/ppermute | solution.py:20
  90.0 2.5 %collective-permute-start.3 = (bf16[2,6,1,256]{3,2,1,0:T(2,128)(2,1)S(1)}, bf16[2,6,1,256]{3,2,1,0:T(2,128)(2,1)S(1)}, u32[]{:S(2)}, u32[]{:S(2)}) collective-permute-start(bf16[2,6,1,256]{3,2,1,0:T(2,128)(2,1)S(1)} %get-tuple-element.148), channel_id=1, source_target_pairs={{1,0},{3,2},{5,4},{7,6},{9,8},{11,10},{13,12},{15,14},{17,16},{19,... | collective-permute-start | bytes 18440 | tf_op jit(solution)/shard_map/ppermute | solution.py:21
  92.5 1.3 %collective-permute-start.2 = (bf16[2,6,1,256]{3,2,1,0:T(2,128)(2,1)S(1)}, bf16[2,6,1,256]{3,2,1,0:T(2,128)(2,1)S(1)}, u32[]{:S(2)}, u32[]{:S(2)}) collective-permute-start(bf16[2,6,1,256]{3,2,1,0:T(2,128)(2,1)S(1)} %get-tuple-element.147), channel_id=1, source_target_pairs={{0,1},{2,3},{4,5},{6,7},{8,9},{10,11},{12,13},{14,15},{16,17},{18,... | collective-permute-start | bytes 18440 | tf_op jit(solution)/shard_map/ppermute | solution.py:20
  93.9 1.3 %collective-permute-start.7 = (f32[2,6,1]{2,1,0:T(8,128)S(1)}, f32[2,6,1]{2,1,0:T(8,128)S(1)}, u32[]{:S(2)}, u32[]{:S(2)}) collective-permute-start(f32[2,6,1]{2,1,0:T(8,128)S(1)} %get-tuple-element.152), channel_id=1, source_target_pairs={{0,1},{2,3},{4,5},{6,7},{8,9},{10,11},{12,13},{14,15},{16,17},{18,... | collective-permute-start | bytes 152 | tf_op jit(solution)/shard_map/ppermute | solution.py:20
  95.2 4.5 %collective-permute-start.6 = (f32[2,6,1]{2,1,0:T(8,128)S(1)}, f32[2,6,1]{2,1,0:T(8,128)S(1)}, u32[]{:S(2)}, u32[]{:S(2)}) collective-permute-start(f32[2,6,1]{2,1,0:T(8,128)S(1)} %get-tuple-element.151), channel_id=1, source_target_pairs={{1,0},{3,2},{5,4},{7,6},{9,8},{11,10},{13,12},{15,14},{17,16},{19,... | collective-permute-start | bytes 152 | tf_op jit(solution)/shard_map/ppermute | solution.py:21
  102.1 1.9 %collective-permute-start.9 = (bf16[3,1,48,256]{3,2,1,0:T(8,128)(2,1)S(1)}, bf16[3,1,48,256]{3,2,1,0:T(8,128)(2,1)S(1)}, u32[]{:S(2)}, u32[]{:S(2)}) collective-permute-start(bf16[3,1,48,256]{3,2,1,0:T(8,128)(2,1)S(1)} %get-tuple-element.146), channel_id=1, source_target_pairs={{2,0},{4,2},{6,4},{8,6},{10,8},{12,10},{14,12},{16,14},{18,16},{20... | collective-permute-start | bytes 221192 | tf_op jit(solution)/shard_map/ppermute | solution.py:21
  104.0 2.4 %collective-permute-start.8 = (bf16[3,1,48,256]{3,2,1,0:T(8,128)(2,1)S(1)}, bf16[3,1,48,256]{3,2,1,0:T(8,128)(2,1)S(1)}, u32[]{:S(2)}, u32[]{:S(2)}) collective-permute-start(bf16[3,1,48,256]{3,2,1,0:T(8,128)(2,1)S(1)} %get-tuple-element.145), channel_id=1, source_target_pairs={{0,2},{2,4},{4,6},{6,8},{8,10},{10,12},{12,14},{14,16},{16,18},{18... | collective-permute-start | bytes 221192 | tf_op jit(solution)/shard_map/ppermute | solution.py:20
  106.6 4.0 %collective-permute-done.8 = bf16[3,1,48,256]{3,2,1,0:T(8,128)(2,1)S(1)} collective-permute-done((bf16[3,1,48,256]{3,2,1,0:T(8,128)(2,1)S(1)}, bf16[3,1,48,256]{3,2,1,0:T(8,128)(2,1)S(1)}, u32[]{:S(2)}, u32[]{:S(2)}) %collective-permute-start.8) | collective-permute-done | bytes 73760 | tf_op jit(solution)/shard_map/ppermute | solution.py:20
  110.6 1.3 %collective-permute-start.11 = (bf16[3,6,1,256]{3,2,1,0:T(2,128)(2,1)S(1)}, bf16[3,6,1,256]{3,2,1,0:T(2,128)(2,1)S(1)}, u32[]{:S(2)}, u32[]{:S(2)}) collective-permute-start(bf16[3,6,1,256]{3,2,1,0:T(2,128)(2,1)S(1)} %get-tuple-element.139), channel_id=1, source_target_pairs={{1,0},{3,2},{5,4},{7,6},{9,8},{11,10},{13,12},{15,14},{17,16},{19,... | collective-permute-start | bytes 27656 | tf_op jit(solution)/shard_map/ppermute | solution.py:21
  111.9 1.3 %collective-permute-start.10 = (bf16[3,6,1,256]{3,2,1,0:T(2,128)(2,1)S(1)}, bf16[3,6,1,256]{3,2,1,0:T(2,128)(2,1)S(1)}, u32[]{:S(2)}, u32[]{:S(2)}) collective-permute-start(bf16[3,6,1,256]{3,2,1,0:T(2,128)(2,1)S(1)} %get-tuple-element.138), channel_id=1, source_target_pairs={{0,1},{2,3},{4,5},{6,7},{8,9},{10,11},{12,13},{14,15},{16,17},{18,... | collective-permute-start | bytes 27656 | tf_op jit(solution)/shard_map/ppermute | solution.py:20
  113.9 3.7 %collective-permute-done.10 = bf16[3,6,1,256]{3,2,1,0:T(2,128)(2,1)S(1)} collective-permute-done((bf16[3,6,1,256]{3,2,1,0:T(2,128)(2,1)S(1)}, bf16[3,6,1,256]{3,2,1,0:T(2,128)(2,1)S(1)}, u32[]{:S(2)}, u32[]{:S(2)}) %collective-permute-start.10) | collective-permute-done | bytes 9248 | tf_op jit(solution)/shard_map/ppermute | solution.py:20
  (74 shorter events, 9.3 us)
Async XLA Ops:
  7.2 52.0 %all-gather.2.cloned.1.call-start = ((), (), s32[]{:S(2)}) async-start(), calls=%async_computation | async-start | bytes 3342336 | tf_op jit(solution)/shard_map/all_gather | solution.py:126
  72.0 12.9 %collective-permute-start.4 = (f32[2,1,48]{2,1,0:T(1,128)S(1)}, f32[2,1,48]{2,1,0:T(1,128)S(1)}, u32[]{:S(2)}, u32[]{:S(2)}) collective-permute-start(f32[2,1,48]{2,1,0:T(1,128)S(1)} %get-tuple-element.154), channel_id=1, source_target_pairs={{2,0},{4,2},{6,4},{8,6},{10,8},{12,10},{14,12},{16,14},{18,16},{20... | collective-permute-start | bytes 1160 | tf_op jit(solution)/shard_map/ppermute | solution.py:21
  75.0 9.9 %collective-permute-start.5 = (f32[2,1,48]{2,1,0:T(1,128)S(1)}, f32[2,1,48]{2,1,0:T(1,128)S(1)}, u32[]{:S(2)}, u32[]{:S(2)}) collective-permute-start(f32[2,1,48]{2,1,0:T(1,128)S(1)} %get-tuple-element.153), channel_id=1, source_target_pairs={{0,2},{2,4},{4,6},{6,8},{8,10},{10,12},{12,14},{14,16},{16,18},{18... | collective-permute-start | bytes 1160 | tf_op jit(solution)/shard_map/ppermute | solution.py:20
  78.4 6.5 %collective-permute-start.1 = (bf16[2,1,48,256]{3,2,1,0:T(8,128)(2,1)S(1)}, bf16[2,1,48,256]{3,2,1,0:T(8,128)(2,1)S(1)}, u32[]{:S(2)}, u32[]{:S(2)}) collective-permute-start(bf16[2,1,48,256]{3,2,1,0:T(8,128)(2,1)S(1)} %get-tuple-element.150), channel_id=1, source_target_pairs={{2,0},{4,2},{6,4},{8,6},{10,8},{12,10},{14,12},{16,14},{18,16},{20... | collective-permute-start | bytes 147464 | tf_op jit(solution)/shard_map/ppermute | solution.py:21
  82.9 6.3 %collective-permute-start = (bf16[2,1,48,256]{3,2,1,0:T(8,128)(2,1)S(1)}, bf16[2,1,48,256]{3,2,1,0:T(8,128)(2,1)S(1)}, u32[]{:S(2)}, u32[]{:S(2)}) collective-permute-start(bf16[2,1,48,256]{3,2,1,0:T(8,128)(2,1)S(1)} %get-tuple-element.149), channel_id=1, source_target_pairs={{0,2},{2,4},{4,6},{6,8},{8,10},{10,12},{12,14},{14,16},{16,18},{18... | collective-permute-start | bytes 147464 | tf_op jit(solution)/shard_map/ppermute | solution.py:20
  90.0 9.7 %collective-permute-start.3 = (bf16[2,6,1,256]{3,2,1,0:T(2,128)(2,1)S(1)}, bf16[2,6,1,256]{3,2,1,0:T(2,128)(2,1)S(1)}, u32[]{:S(2)}, u32[]{:S(2)}) collective-permute-start(bf16[2,6,1,256]{3,2,1,0:T(2,128)(2,1)S(1)} %get-tuple-element.148), channel_id=1, source_target_pairs={{1,0},{3,2},{5,4},{7,6},{9,8},{11,10},{13,12},{15,14},{17,16},{19,... | collective-permute-start | bytes 18440 | tf_op jit(solution)/shard_map/ppermute | solution.py:21
  92.5 7.2 %collective-permute-start.2 = (bf16[2,6,1,256]{3,2,1,0:T(2,128)(2,1)S(1)}, bf16[2,6,1,256]{3,2,1,0:T(2,128)(2,1)S(1)}, u32[]{:S(2)}, u32[]{:S(2)}) collective-permute-start(bf16[2,6,1,256]{3,2,1,0:T(2,128)(2,1)S(1)} %get-tuple-element.147), channel_id=1, source_target_pairs={{0,1},{2,3},{4,5},{6,7},{8,9},{10,11},{12,13},{14,15},{16,17},{18,... | collective-permute-start | bytes 18440 | tf_op jit(solution)/shard_map/ppermute | solution.py:20
  93.9 12.7 %collective-permute-start.7 = (f32[2,6,1]{2,1,0:T(8,128)S(1)}, f32[2,6,1]{2,1,0:T(8,128)S(1)}, u32[]{:S(2)}, u32[]{:S(2)}) collective-permute-start(f32[2,6,1]{2,1,0:T(8,128)S(1)} %get-tuple-element.152), channel_id=1, source_target_pairs={{0,1},{2,3},{4,5},{6,7},{8,9},{10,11},{12,13},{14,15},{16,17},{18,... | collective-permute-start | bytes 152 | tf_op jit(solution)/shard_map/ppermute | solution.py:20
  95.2 11.4 %collective-permute-start.6 = (f32[2,6,1]{2,1,0:T(8,128)S(1)}, f32[2,6,1]{2,1,0:T(8,128)S(1)}, u32[]{:S(2)}, u32[]{:S(2)}) collective-permute-start(f32[2,6,1]{2,1,0:T(8,128)S(1)} %get-tuple-element.151), channel_id=1, source_target_pairs={{1,0},{3,2},{5,4},{7,6},{9,8},{11,10},{13,12},{15,14},{17,16},{19,... | collective-permute-start | bytes 152 | tf_op jit(solution)/shard_map/ppermute | solution.py:21
  102.1 4.5 %collective-permute-start.9 = (bf16[3,1,48,256]{3,2,1,0:T(8,128)(2,1)S(1)}, bf16[3,1,48,256]{3,2,1,0:T(8,128)(2,1)S(1)}, u32[]{:S(2)}, u32[]{:S(2)}) collective-permute-start(bf16[3,1,48,256]{3,2,1,0:T(8,128)(2,1)S(1)} %get-tuple-element.146), channel_id=1, source_target_pairs={{2,0},{4,2},{6,4},{8,6},{10,8},{12,10},{14,12},{16,14},{18,16},{20... | collective-permute-start | bytes 221192 | tf_op jit(solution)/shard_map/ppermute | solution.py:21
  104.0 6.6 %collective-permute-start.8 = (bf16[3,1,48,256]{3,2,1,0:T(8,128)(2,1)S(1)}, bf16[3,1,48,256]{3,2,1,0:T(8,128)(2,1)S(1)}, u32[]{:S(2)}, u32[]{:S(2)}) collective-permute-start(bf16[3,1,48,256]{3,2,1,0:T(8,128)(2,1)S(1)} %get-tuple-element.145), channel_id=1, source_target_pairs={{0,2},{2,4},{4,6},{6,8},{8,10},{10,12},{12,14},{14,16},{16,18},{18... | collective-permute-start | bytes 221192 | tf_op jit(solution)/shard_map/ppermute | solution.py:20
  110.6 3.3 %collective-permute-start.11 = (bf16[3,6,1,256]{3,2,1,0:T(2,128)(2,1)S(1)}, bf16[3,6,1,256]{3,2,1,0:T(2,128)(2,1)S(1)}, u32[]{:S(2)}, u32[]{:S(2)}) collective-permute-start(bf16[3,6,1,256]{3,2,1,0:T(2,128)(2,1)S(1)} %get-tuple-element.139), channel_id=1, source_target_pairs={{1,0},{3,2},{5,4},{7,6},{9,8},{11,10},{13,12},{15,14},{17,16},{19,... | collective-permute-start | bytes 27656 | tf_op jit(solution)/shard_map/ppermute | solution.py:21
  111.9 5.7 %collective-permute-start.10 = (bf16[3,6,1,256]{3,2,1,0:T(2,128)(2,1)S(1)}, bf16[3,6,1,256]{3,2,1,0:T(2,128)(2,1)S(1)}, u32[]{:S(2)}, u32[]{:S(2)}) collective-permute-start(bf16[3,6,1,256]{3,2,1,0:T(2,128)(2,1)S(1)} %get-tuple-element.138), channel_id=1, source_target_pairs={{0,1},{2,3},{4,5},{6,7},{8,9},{10,11},{12,13},{14,15},{16,17},{18,... | collective-permute-start | bytes 27656 | tf_op jit(solution)/shard_map/ppermute | solution.py:20
  113.9 3.9 %copy-start = (bf16[192,256]{1,0:T(8,128)(2,1)S(1)}, bf16[192,256]{1,0:T(8,128)(2,1)}, u32[]{:S(2)}) copy-start(bf16[192,256]{1,0:T(8,128)(2,1)} %get-tuple-element.280) | copy-start | bytes 294916
Sparse Core Ops, SparseCore 0:
  13.2 45.9 all-gather.1
where the time goes:
time: 126 us
  waiting for transfers between devices  57.8 us (46%)
  starting transfers between devices  27.9 us (22%)
  between operations  14.4 us (11%)
  matrix products  10.4 us (8%)
  other arithmetic  8.62 us (7%)
  blocking collectives  5.8 us (5%)
    all_gather x1, waiting for transfers between devices, body(): piece = lax.all_gather(band, 'blk', axis=0, tiled=True)  45.7 us
    ppermute x6, starting transfers between devices, with_halo(): after = lax.ppermute(first, axis, down)  17.7 us
    ppermute x6, waiting for transfers between devices, with_halo(): before = lax.ppermute(last, axis, up)  12 us
    ppermute x6, starting transfers between devices, with_halo(): before = lax.ppermute(last, axis, up)  10.1 us
    all_gather x1, blocking collectives, body(): band = lax.all_gather(feat2, 'col', axis=1, tiled=True)  5.8 us
    dot_general x3, matrix products, visit(): lax.dot_general(queries, key_block, (((1,), (1,)), ((), ())), preferred_e...  5.46 us
    dot_general x3, matrix products, visit(): jnp.dot(expo.astype(jnp.bfloat16), key_block, preferred_element_type=jnp....  4.97 us
  transfers between devices with their start and end apart: 13, of which 4 were waited for; matrix products, arithmetic and copies ran while one was open for 4% of the time, Pallas kernels for 0%

commit v1 on v0

v1 whole, which is shorter than its diff:
```python
import functools
import math

import jax
import jax.numpy as jnp
from jax import lax
from jax.experimental import pallas as pl
from jax.experimental.pallas import tpu as pltpu
from jax.sharding import PartitionSpec as P

ssim_one = 0.01
ssim_two = 0.03
charb_sq = 0.0001
SIDE = 8
MESH = pl.DeviceIdType.MESH


def gather_attend(
    nblk, ncol, f1, f2, x_out, y_out, c_out,
    keys, top_h, bot_h, left_h, right_h, xext, peak, acc, acc_c,
    recv, send_z, send_x, send_y, send_c, halo_send, halo_recv,
):
    rows, cols, width = f1.shape
    half_rows = rows // 2
    nz = nblk // 4
    i = lax.axis_index("blk")
    y = lax.axis_index("col")
    c = lax.rem(i, 2)
    x = lax.rem(i // 2, 2)
    z = i // 4

    def blk_of(zz, xx, cc):
        return (zz * 2 + xx) * 2 + cc

    def zmod(k):
        return lax.rem(z + k, nz)

    def ymod(k):
        return lax.rem(y + k, ncol)

    other_x = (blk_of(z, 1 - x, c), y)
    sibling = (blk_of(z, x, 1 - c), y)
    up, down = lax.rem(i + nblk - 1, nblk), lax.rem(i + 1, nblk)
    west, east = ymod(ncol - 1), ymod(1)

    keys[y, i] = f2[...]

    around = [(up, y), (down, y), (i, west), (i, east), (up, west), (up, east), (down, west), (down, east)]
    peers = [(blk_of(zmod(k), x, c), y) for k in range(1, nz)]
    peers += [(i, ymod(k)) for k in range(1, ncol)]
    peers += [other_x, sibling] + around
    barrier = pltpu.get_barrier_semaphore()
    for peer in peers:
        pl.semaphore_signal(barrier, inc=1, device_id=peer, device_id_type=MESH)
    pl.semaphore_wait(barrier, len(peers))

    def copy(yy, b, half, dest, sem):
        part = keys.at[yy, b, pl.ds(half * half_rows, half_rows)]
        return pltpu.make_async_remote_copy(
            src_ref=part, dst_ref=part, send_sem=sem, recv_sem=recv.at[yy, b, half],
            device_id=dest, device_id_type=MESH,
        )

    def arrived(yy, b, half):
        copy(yy, b, half, sibling, send_c.at[yy, b // 2, half]).wait_recv()

    def z_copy(k, half):
        return copy(y, i, half, (blk_of(zmod(k), x, c), y), send_z.at[k - 1, half])

    def x_copy(yy, zz, half):
        return copy(yy, blk_of(zz, x, c), half, other_x, send_x.at[half, yy, zz])

    def y_copy(k, zz, xx, half):
        return copy(y, blk_of(zz, xx, c), half, (i, ymod(k)), send_y.at[half, k - 1, zz, xx])

    def c_copy(yy, zz, xx, half):
        return copy(yy, blk_of(zz, xx, c), half, sibling, send_c.at[yy, zz * 2 + xx, half])

    def y_range(fn):
        if ncol == 2:
            fn(1)
        else:
            lax.fori_loop(1, ncol, lambda k, u: (fn(k), u)[1], 0)

    def z_range(low, fn):
        lax.fori_loop(low, nz, lambda k, u: (fn(k), u)[1], 0)

    def start_column(zz):
        x_copy(y, zz, 0).start()
        y_range(lambda k: y_copy(k, zz, x, 1).start())
        x_copy(y, zz, 1).start()
        y_range(lambda k: y_copy(k, zz, x, 0).start())
        c_copy(y, zz, x, 0).start()
        c_copy(y, zz, x, 1).start()

    def halo(src, dst, dest, n):
        return pltpu.make_async_remote_copy(
            src_ref=src, dst_ref=dst, send_sem=halo_send.at[n], recv_sem=halo_recv.at[n],
            device_id=dest, device_id_type=MESH,
        )

    first, last = pl.ds(0, 2), pl.ds(rows - 2, 2)
    lead, tail = pl.ds(0, 16), pl.ds(cols - 16, 16)
    mid, end = pl.ds(2, rows), pl.ds(rows + 2, 2)
    halos = [
        halo(f1.at[last], top_h, (down, y), 0),
        halo(f1.at[first], bot_h, (up, y), 1),
        halo(f1.at[:, tail], left_h.at[mid], (i, east), 2),
        halo(f1.at[:, lead], right_h.at[mid], (i, west), 3),
        halo(f1.at[last, tail], left_h.at[first], (down, east), 4),
        halo(f1.at[last, lead], right_h.at[first], (down, west), 5),
        halo(f1.at[first, tail], left_h.at[end], (up, east), 6),
        halo(f1.at[first, lead], right_h.at[end], (up, west), 7),
    ]

    for k in range(1, nz):
        z_copy(k, 0).start()
        z_copy(k, 1).start()
    for item in halos:
        item.start()
    start_column(z)

    peak[...] = jnp.full_like(peak, -1e30)
    acc[...] = jnp.zeros_like(acc)
    acc_c[...] = jnp.zeros_like(acc_c)
    per = 2 * rows * cols
    where = lax.broadcasted_iota(jnp.int32, (2 * rows, cols, 128), 0)
    along = lax.broadcasted_iota(jnp.int32, (2 * rows, cols, 128), 1)
    lane = lax.broadcasted_iota(jnp.int32, (2 * rows, cols, 128), 2)
    pattern = jnp.where(lane == 0, 1, jnp.where(lane == 1, where, jnp.where(lane == 2, along, 0)))
    pattern = pattern.astype(jnp.float32).reshape(per, 128)
    lane_row = lax.broadcasted_iota(jnp.int32, (1, 128), 1)

    for item in halos:
        item.wait_recv()
    xext[0:2, 0:cols] = top_h[...].astype(jnp.float32)
    xext[2 : rows + 2, 0:cols] = f1[...].astype(jnp.float32)
    xext[rows + 2 : rows + 4, 0:cols] = bot_h[...].astype(jnp.float32)
    spot = lax.broadcasted_iota(jnp.int32, (rows + 4, SIDE, width), 1)
    xext[:, cols : cols + SIDE] = jnp.where(
        spot < SIDE // 2,
        right_h[...].astype(jnp.float32)[:, 0:SIDE],
        left_h[...].astype(jnp.float32)[:, 16 - SIDE : 16],
    )
    count = (rows + 4) * (cols + SIDE)
    x_out[...] = xext[...].reshape(count, width).astype(jnp.bfloat16)
    scale = 1.0 / math.sqrt(width)

    def absorb(yy, zz, xx):
        chip = zz * 2 + xx
        for half in range(2):
            arrived(yy, chip * 2 + 1 - c, half)
        block = keys[yy, pl.ds(chip * 2, 2)].reshape(per, width)
        base = jnp.where(lane_row == 1, chip * 2 * rows, jnp.where(lane_row == 3, yy, 0))
        coords = (pattern + base.astype(jnp.float32)).astype(jnp.bfloat16)
        score = lax.dot_general(
            x_out[...], block, (((1,), (1,)), ((), ())), preferred_element_type=jnp.float32
        ) * scale
        old = peak[...]
        new = jnp.maximum(old, jnp.max(score, axis=1, keepdims=True))
        peak[...] = new
        shrink = jnp.exp(old - new)
        full = jnp.exp(score - new[:, 0:1])
        expo = full.astype(jnp.bfloat16)
        rest = (full - expo.astype(jnp.float32)).astype(jnp.bfloat16)
        acc[...] = acc[...] * shrink[:, 0:1] + jnp.dot(expo, block, preferred_element_type=jnp.float32)
        acc_c[...] = (
            acc_c[...] * shrink
            + jnp.dot(expo, coords, preferred_element_type=jnp.float32)
            + jnp.dot(rest, coords, preferred_element_type=jnp.float32)
        )

    absorb(y, z, x)

    def wave_z(k):
        zz = zmod(k)
        arrived(y, blk_of(zz, x, c), 0)
        arrived(y, blk_of(zz, x, c), 1)
        start_column(zz)

    z_range(1, wave_z)

    def wave_one(k):
        zz = zmod(k)
        arrived(y, blk_of(zz, 1 - x, c), 0)
        y_range(lambda j: y_copy(j, zz, 1 - x, 0).start())
        c_copy(y, zz, 1 - x, 0).start()

        def take(j):
            yy = ymod(j)
            arrived(yy, blk_of(zz, x, c), 1)
            x_copy(yy, zz, 1).start()
            c_copy(yy, zz, x, 1).start()

        y_range(take)

        @pl.when(k > 0)
        def _():
            absorb(y, zz, x)

    z_range(0, wave_one)

    def wave_two(k):
        zz = zmod(k)
        arrived(y, blk_of(zz, 1 - x, c), 1)
        c_copy(y, zz, 1 - x, 1).start()

        def take(j):
            yy = ymod(j)
            arrived(yy, blk_of(zz, x, c), 0)
            c_copy(yy, zz, x, 0).start()

        y_range(take)

        @pl.when(k > 0)
        def _():
            absorb(y, zmod(k + nz - 1), 1 - x)
            y_range(lambda j: absorb(ymod(j), zmod(k + nz - 1), x))

    z_range(0, wave_two)

    def wave_three(k):
        zz = zmod(k)

        def take(j):
            yy = ymod(j)
            arrived(yy, blk_of(zz, 1 - x, c), 0)
            c_copy(yy, zz, 1 - x, 0).start()
            arrived(yy, blk_of(zz, 1 - x, c), 1)
            c_copy(yy, zz, 1 - x, 1).start()

        y_range(take)

        @pl.when(k == 0)
        def _():
            absorb(y, zmod(nz - 1), 1 - x)
            y_range(lambda j: absorb(ymod(j), zmod(nz - 1), x))

        @pl.when(k > 0)
        def _():
            y_range(lambda j: absorb(ymod(j), zmod(k + nz - 1), 1 - x))

    z_range(0, wave_three)
    y_range(lambda j: absorb(ymod(j), zmod(nz - 1), 1 - x))

    total = acc_c[:, 0:1]
    y_out[...] = (acc[...] / total).astype(jnp.bfloat16)
    c_out[...] = acc_c[...] / total

    for item in halos:
        item.wait_send()
    for k in range(1, nz):
        z_copy(k, 0).wait_send()
        z_copy(k, 1).wait_send()

    def drain(zz):
        x_copy(y, zz, 0).wait_send()
        x_copy(y, zz, 1).wait_send()
        for xx in range(2):
            c_copy(y, zz, xx, 0).wait_send()
            c_copy(y, zz, xx, 1).wait_send()

        def each(j):
            yy = ymod(j)
            x_copy(yy, zz, 1).wait_send()
            y_copy(j, zz, x, 1).wait_send()
            for xx in range(2):
                y_copy(j, zz, xx, 0).wait_send()
                c_copy(yy, zz, xx, 0).wait_send()
                c_copy(yy, zz, xx, 1).wait_send()

        y_range(each)

    z_range(0, drain)


def col_sum(v):
    size = v.shape[1]
    return v + pltpu.roll(v, 1, 1) + pltpu.roll(v, size - 1, 1)


def box(v):
    n = v.shape[0]
    return col_sum(v[0 : n - 2] + v[1 : n - 1] + v[2:n]) * (1.0 / 9.0)


def turn(v, step):
    if step == 1:
        return jnp.concatenate([v[:, -1:], v[:, :-1]], axis=1)
    return jnp.concatenate([v[:, 1:], v[:, :1]], axis=1)


def charbonnier(weight, delta):
    return weight * delta / jnp.sqrt(delta * delta + charb_sq)


def stencil(nblk, ncol, rows, cols, x_ref, y_ref, c_ref, flow_ref, gflow_ref, grad_ref):
    width = x_ref.shape[1]
    span = cols + SIDE
    i = lax.axis_index("blk")
    y = lax.axis_index("col")
    full_rows, full_cols = rows * nblk, cols * ncol

    def place(shape, row_axis, col_axis, first_row):
        r = lax.broadcasted_iota(jnp.int32, shape, row_axis) + (i * rows + first_row)
        w = lax.broadcasted_iota(jnp.int32, shape, col_axis)
        w = jnp.where(w >= cols + SIDE // 2, w - span, w) + y * cols
        return r, w

    def inside(shape, first_row):
        r, w = place(shape, 0, 1, first_row)
        return (r >= 0) & (r < full_rows) & (w >= 0) & (w < full_cols)

    xraw = x_ref[...].astype(jnp.float32).reshape(rows + 4, span, width)
    keep = inside(xraw.shape, -2)
    xv = jnp.where(keep, xraw, 0.0)
    yv = jnp.where(keep, y_ref[...].astype(jnp.float32).reshape(rows + 4, span, width), 0.0)
    mx, my = box(xv), box(yv)
    vx = box(xv * xv) - mx * mx
    vy = box(yv * yv) - my * my
    cv = box(xv * yv) - mx * my
    n1 = 2.0 * mx * my + ssim_one
    n2 = 2.0 * cv + ssim_two
    d1 = mx * mx + my * my + ssim_one
    d2 = vx + vy + ssim_two
    inv1 = 1.0 / d1
    inv2 = 1.0 / d2
    inv = inv1 * inv2
    ssim = n1 * n2 * inv
    a = ssim * my * inv1 - mx * n2 * inv
    b = 0.5 * ssim * inv2
    cc = -n1 * inv
    first = a - 2.0 * b * my - cc * mx
    ok = inside(mx.shape, -1)
    g1 = box(jnp.where(ok, first, 0.0))
    g2 = box(jnp.where(ok, b, 0.0))
    g3 = box(jnp.where(ok, cc, 0.0))
    yc = yv[2 : rows + 2]
    xc = xv[2 : rows + 2]
    grad_ref[...] = (g1 + 2.0 * yc * g2 + xc * g3)[:, 0:cols]

    sums = jnp.transpose(c_ref[...])

    def plane(n):
        line = sums[n : n + 1]
        return jnp.concatenate([line[:, r * span : (r + 1) * span] for r in range(rows + 4)], axis=0)

    rr, ww = place((rows + 4, span), 0, 1, -2)
    fy = (plane(1) + 0.5) * (2.0 / full_rows) - 1.0 - ((rr.astype(jnp.float32) + 0.5) * (2.0 / full_rows) - 1.0)
    px = plane(2) + plane(3) * float(cols)
    fx = (px + 0.5) * (2.0 / full_cols) - 1.0 - ((ww.astype(jnp.float32) + 0.5) * (2.0 / full_cols) - 1.0)
    flow_ref[0] = fy[2 : rows + 2, 0:cols]
    flow_ref[1] = fx[2 : rows + 2, 0:cols]

    w_y = jnp.exp(-jnp.mean(jnp.abs(xraw[2 : rows + 3] - xraw[1 : rows + 2]), axis=-1))
    mid = xraw[2 : rows + 2]
    w_x = jnp.exp(-jnp.mean(jnp.abs(mid - pltpu.roll(mid, 1, 1)), axis=-1))
    er, _ = place((rows + 1, span), 0, 1, -1)
    use_y = (er >= 0) & (er <= full_rows - 2)
    _, ew = place((rows, span), 0, 1, 0)
    use_x = (ew >= 1) & (ew <= full_cols - 1)
    for n, f in enumerate((fy, fx)):
        push_y = jnp.where(use_y, charbonnier(w_y, f[2 : rows + 3] - f[1 : rows + 2]), 0.0)
        fm = f[2 : rows + 2]
        push_x = jnp.where(use_x, charbonnier(w_x, fm - turn(fm, 1)), 0.0)
        out = push_y[0:rows] - push_y[1 : rows + 1] + push_x - turn(push_x, -1)
        gflow_ref[n] = out[:, 0:cols]


def body(nblk, ncol, feat1, feat2):
    rows, cols, width = feat1.shape
    nz = nblk // 4
    count = (rows + 4) * (cols + SIDE)
    vmem = pl.BlockSpec(memory_space=pltpu.VMEM)
    dma = pltpu.SemaphoreType.DMA
    bf = jnp.bfloat16
    xq, warped, sums = pl.pallas_call(
        functools.partial(gather_attend, nblk, ncol),
        out_shape=(
            jax.ShapeDtypeStruct((count, width), bf),
            jax.ShapeDtypeStruct((count, width), bf),
            jax.ShapeDtypeStruct((count, 128), jnp.float32),
        ),
        in_specs=[vmem] * 2,
        out_specs=(vmem, vmem, vmem),
        scratch_shapes=[
            pltpu.VMEM((ncol, nblk, rows, cols, width), bf),
            pltpu.VMEM((2, cols, width), bf),
            pltpu.VMEM((2, cols, width), bf),
            pltpu.VMEM((rows + 4, 16, width), bf),
            pltpu.VMEM((rows + 4, 16, width), bf),
            pltpu.VMEM((rows + 4, cols + SIDE, width), jnp.float32),
            pltpu.VMEM((count, 128), jnp.float32),
            pltpu.VMEM((count, width), jnp.float32),
            pltpu.VMEM((count, 128), jnp.float32),
            dma((ncol, nblk, 2)),
            dma((nz - 1, 2)),
            dma((2, ncol, nz)),
            dma((2, ncol - 1, nz, 2)),
            dma((ncol, nblk // 2, 2)),
            dma((8,)),
            dma((8,)),
        ],
        compiler_params=pltpu.CompilerParams(
            collective_id=0, has_side_effects=True, vmem_limit_bytes=48 * 1024 * 1024
        ),
    )(feat1, feat2)
    return pl.pallas_call(
        functools.partial(stencil, nblk, ncol, rows, cols),
        out_shape=(
            jax.ShapeDtypeStruct((2, rows, cols), jnp.float32),
            jax.ShapeDtypeStruct((2, rows, cols), jnp.float32),
            jax.ShapeDtypeStruct((rows, cols, width), jnp.float32),
        ),
        in_specs=[vmem] * 3,
        out_specs=(vmem, vmem, vmem),
        compiler_params=pltpu.CompilerParams(vmem_limit_bytes=40 * 1024 * 1024),
    )(xq, warped, sums)


def solution(mesh):
    placed = (P("blk", "col", None), P("blk", "col", None))
    return jax.shard_map(
        functools.partial(body, mesh.shape["blk"], mesh.shape["col"]),
        mesh=mesh,
        in_specs=placed,
        out_specs=(P(None, "blk", "col"), P(None, "blk", "col"), P("blk", "col", None)),
        check_vma=False,
    )
```

time: 126 us -> 46.3 us (0.37)
  the two profiles are of different devices: /device:TPU:20 before, /device:TPU:0 now
where the time goes in v1:
time: 46.3 us; the launch traced here: 46.1 us
  Pallas kernels  43.7 us (94%)
  local copies, waits for them, and re-layouts  1.78 us (4%)
  between operations  0.65 us (1%)
    pallas_call x1, Pallas kernels, body(): pl.pallas_call(functools.partial(gather_attend, nblk, ncol), out_shape=(j...  41 us
    pallas_call x1, Pallas kernels, body(): pl.pallas_call(functools.partial(stencil, nblk, ncol, rows, cols), out_sh...  2.67 us
    unnamed x4, local copies, waits for them, and re-layouts  1.78 us

profile of v1, /device:TPU:0, one launch (start us, length us, event | category | flops | bytes accessed | tf_op | source)
XLA Modules:
  0.0 46.1 jit_solution(11852167987511462357)
XLA Ops:
  0.6 0.0 copy-start
  0.6 0.9 %copy-done = bf16[4,48,256]{2,1,0:T(8,128)(2,1)S(1)} copy-done((bf16[4,48,256]{2,1,0:T(8,128)(2,1)S(1)}, bf16[4,48,256]{2,1,0:T(8,128)(2,1)}, u32[]{:S(2)}) %copy-start) | copy-done | bytes 98328
  1.5 0.0 copy-start.1
  1.5 0.9 %copy-done.1 = bf16[4,48,256]{2,1,0:T(8,128)(2,1)S(1)} copy-done((bf16[4,48,256]{2,1,0:T(8,128)(2,1)S(1)}, bf16[4,48,256]{2,1,0:T(8,128)(2,1)}, u32[]{:S(2)}) %copy-start.1) | copy-done | bytes 98328
  2.4 41.0 %shard_map.49 = (bf16[448,256]{1,0:T(8,128)(2,1)S(1)}, bf16[448,256]{1,0:T(8,128)(2,1)S(1)}, f32[448,128]{1,0:T(8,128)S(1)}) custom-call(bf16[4,48,256]{2,1,0:T(8,128)(2,1)S(1)} %copy-done, bf16[4,48,256]{2,1,0:T(8,128)(2,1)S(1)} %copy-done.1), custom_call_target="tpu_custom_call" | custom-call | tf_op jit(solution)/shard_map/pallas_call | solution.py:377
  43.4 2.7 %shard_map.50 = (f32[2,4,48]{2,1,0:T(4,128)}, f32[2,4,48]{2,1,0:T(4,128)}, f32[4,48,256]{2,1,0:T(8,128)}) custom-call(bf16[448,256]{1,0:T(8,128)(2,1)S(1)} %get-tuple-element.6.x_ref, bf16[448,256]{1,0:T(8,128)(2,1)S(1)} %get-tuple-element.7.y_ref, f32[448,128]{1,0:T(8,128)S(1)} %get-tuple-element.8.c_ref), custom_call_target="tpu_custom_call" | custom-call | tf_op jit(solution)/shard_map/pallas_call | solution.py:408
Async XLA Ops:
  0.6 0.9 %copy-start = (bf16[4,48,256]{2,1,0:T(8,128)(2,1)S(1)}, bf16[4,48,256]{2,1,0:T(8,128)(2,1)}, u32[]{:S(2)}) copy-start(bf16[4,48,256]{2,1,0:T(8,128)(2,1)} %f1.1) | copy-start | bytes 294916
  1.5 0.9 %copy-start.1 = (bf16[4,48,256]{2,1,0:T(8,128)(2,1)S(1)}, bf16[4,48,256]{2,1,0:T(8,128)(2,1)}, u32[]{:S(2)}) copy-start(bf16[4,48,256]{2,1,0:T(8,128)(2,1)} %f2.1) | copy-start | bytes 294916

commit v2 on v1

--- a/solution.py
+++ b/solution.py
@@ -17,7 +17,7 @@
 
 def gather_attend(
     nblk, ncol, f1, f2, x_out, y_out, c_out,
-    keys, top_h, bot_h, left_h, right_h, xext, peak, acc, acc_c,
+    keys, x_bufs, y_bufs, c_bufs, own_y, own_c, query, ext, ext_c, peak, acc, acc_c,
     recv, send_z, send_x, send_y, send_c, halo_send, halo_recv,
 ):
     rows, cols, width = f1.shape
@@ -102,16 +102,26 @@
     first, last = pl.ds(0, 2), pl.ds(rows - 2, 2)
     lead, tail = pl.ds(0, 16), pl.ds(cols - 16, 16)
     mid, end = pl.ds(2, rows), pl.ds(rows + 2, 2)
-    halos = [
-        halo(f1.at[last], top_h, (down, y), 0),
-        halo(f1.at[first], bot_h, (up, y), 1),
-        halo(f1.at[:, tail], left_h.at[mid], (i, east), 2),
-        halo(f1.at[:, lead], right_h.at[mid], (i, west), 3),
-        halo(f1.at[last, tail], left_h.at[first], (down, east), 4),
-        halo(f1.at[last, lead], right_h.at[first], (down, west), 5),
-        halo(f1.at[first, tail], left_h.at[end], (up, east), 6),
-        halo(f1.at[first, lead], right_h.at[end], (up, west), 7),
-    ]
+    def eight(src, bufs, at):
+        top_h, bot_h, left_h, right_h = bufs
+        return [
+            halo(src.at[last], top_h, (down, y), at),
+            halo(src.at[first], bot_h, (up, y), at + 1),
+            halo(src.at[:, tail], left_h.at[mid], (i, east), at + 2),
+            halo(src.at[:, lead], right_h.at[mid], (i, west), at + 3),
+            halo(src.at[last, tail], left_h.at[first], (down, east), at + 4),
+            halo(src.at[last, lead], right_h.at[first], (down, west), at + 5),
+            halo(src.at[first, tail], left_h.at[end], (up, east), at + 6),
+            halo(src.at[first, lead], right_h.at[end], (up, west), at + 7),
+        ]
+
+    halos = eight(f1, x_bufs, 0)
+    late = [
+        halo(own_c.at[pl.ds(rows - 1, 1)], c_bufs[0], (down, y), 16),
+        halo(own_c.at[pl.ds(0, 1)], c_bufs[1], (up, y), 17),
+        halo(own_c.at[:, pl.ds(cols - SIDE, SIDE)], c_bufs[2], (i, east), 18),
+        halo(own_c.at[:, pl.ds(0, SIDE)], c_bufs[3], (i, west), 19),
+    ] + eight(own_y, y_bufs, 8)
 
     for k in range(1, nz):
         z_copy(k, 0).start()
@@ -131,46 +141,64 @@
     pattern = pattern.astype(jnp.float32).reshape(per, 128)
     lane_row = lax.broadcasted_iota(jnp.int32, (1, 128), 1)
 
-    for item in halos:
-        item.wait_recv()
-    xext[0:2, 0:cols] = top_h[...].astype(jnp.float32)
-    xext[2 : rows + 2, 0:cols] = f1[...].astype(jnp.float32)
-    xext[rows + 2 : rows + 4, 0:cols] = bot_h[...].astype(jnp.float32)
-    spot = lax.broadcasted_iota(jnp.int32, (rows + 4, SIDE, width), 1)
-    xext[:, cols : cols + SIDE] = jnp.where(
-        spot < SIDE // 2,
-        right_h[...].astype(jnp.float32)[:, 0:SIDE],
-        left_h[...].astype(jnp.float32)[:, 16 - SIDE : 16],
-    )
     count = (rows + 4) * (cols + SIDE)
-    x_out[...] = xext[...].reshape(count, width).astype(jnp.bfloat16)
     scale = 1.0 / math.sqrt(width)
-
-    def absorb(yy, zz, xx):
-        chip = zz * 2 + xx
-        for half in range(2):
-            arrived(yy, chip * 2 + 1 - c, half)
-        block = keys[yy, pl.ds(chip * 2, 2)].reshape(per, width)
-        base = jnp.where(lane_row == 1, chip * 2 * rows, jnp.where(lane_row == 3, yy, 0))
-        coords = (pattern + base.astype(jnp.float32)).astype(jnp.bfloat16)
-        score = lax.dot_general(
-            x_out[...], block, (((1,), (1,)), ((), ())), preferred_element_type=jnp.float32
-        ) * scale
+    query[...] = (f1[...].astype(jnp.float32) * scale).reshape(rows * cols, width).astype(jnp.bfloat16)
+
+    def widen(own, bufs):
+        top_h, bot_h, left_h, right_h = bufs
+        ext[0:2, 0:cols] = top_h[...].astype(jnp.float32)
+        ext[2 : rows + 2, 0:cols] = own[...].astype(jnp.float32)
+        ext[rows + 2 : rows + 4, 0:cols] = bot_h[...].astype(jnp.float32)
+        spot = lax.broadcasted_iota(jnp.int32, (rows + 4, SIDE, width), 1)
+        ext[:, cols : cols + SIDE] = jnp.where(
+            spot < SIDE // 2,
+            right_h[...].astype(jnp.float32)[:, 0:SIDE],
+            left_h[...].astype(jnp.float32)[:, 16 - SIDE : 16],
+        )
+        return ext[...].reshape(count, width).astype(jnp.bfloat16)
+
+    def absorb(*chips):
+        blocks, coords, scores = [], [], []
+        for yy, zz, xx in chips:
+            chip = zz * 2 + xx
+            for half in range(2):
+                arrived(yy, chip * 2 + 1 - c, half)
+            block = keys[yy, pl.ds(chip * 2, 2)].reshape(per, width)
+            base = jnp.where(lane_row == 1, chip * 2 * rows, jnp.where(lane_row == 3, yy, 0))
+            blocks.append(block)
+            coords.append((pattern + base.astype(jnp.float32)).astype(jnp.bfloat16))
+            scores.append(
+                lax.dot_general(
+                    query[...], block, (((1,), (1,)), ((), ())), preferred_element_type=jnp.float32
+                )
+            )
         old = peak[...]
-        new = jnp.maximum(old, jnp.max(score, axis=1, keepdims=True))
+        new = old
+        for score in scores:
+            new = jnp.maximum(new, jnp.max(score, axis=1, keepdims=True))
         peak[...] = new
         shrink = jnp.exp(old - new)
-        full = jnp.exp(score - new[:, 0:1])
-        expo = full.astype(jnp.bfloat16)
-        rest = (full - expo.astype(jnp.float32)).astype(jnp.bfloat16)
-        acc[...] = acc[...] * shrink[:, 0:1] + jnp.dot(expo, block, preferred_element_type=jnp.float32)
-        acc_c[...] = (
-            acc_c[...] * shrink
-            + jnp.dot(expo, coords, preferred_element_type=jnp.float32)
-            + jnp.dot(rest, coords, preferred_element_type=jnp.float32)
-        )
-
-    absorb(y, z, x)
+        mixed = acc[...] * shrink[:, 0:1]
+        placed = acc_c[...] * shrink
+        for block, coord, score in zip(blocks, coords, scores):
+            full = jnp.exp(score - new[:, 0:1])
+            expo = full.astype(jnp.bfloat16)
+            rest = (full - expo.astype(jnp.float32)).astype(jnp.bfloat16)
+            mixed = mixed + jnp.dot(expo, block, preferred_element_type=jnp.float32)
+            placed = placed + jnp.dot(expo, coord, preferred_element_type=jnp.float32)
+            placed = placed + jnp.dot(rest, coord, preferred_element_type=jnp.float32)
+        acc[...] = mixed
+        acc_c[...] = placed
+
+    def absorb_two(zz):
+        if ncol == 2:
+            absorb((y, zz, 1 - x), (1 - y, zz, x))
+        else:
+            absorb((y, zz, 1 - x))
+            y_range(lambda j: absorb((ymod(j), zz, x)))
+
+    absorb((y, z, x))
 
     def wave_z(k):
         zz = zmod(k)
@@ -196,7 +224,7 @@
 
         @pl.when(k > 0)
         def _():
-            absorb(y, zz, x)
+            absorb((y, zz, x))
 
     z_range(0, wave_one)
 
@@ -214,8 +242,7 @@
 
         @pl.when(k > 0)
         def _():
-            absorb(y, zmod(k + nz - 1), 1 - x)
-            y_range(lambda j: absorb(ymod(j), zmod(k + nz - 1), x))
+            absorb_two(zmod(k + nz - 1))
 
     z_range(0, wave_two)
 
@@ -233,20 +260,38 @@
 
         @pl.when(k == 0)
         def _():
-            absorb(y, zmod(nz - 1), 1 - x)
-            y_range(lambda j: absorb(ymod(j), zmod(nz - 1), x))
+            absorb_two(zmod(nz - 1))
 
         @pl.when(k > 0)
         def _():
-            y_range(lambda j: absorb(ymod(j), zmod(k + nz - 1), 1 - x))
+            y_range(lambda j: absorb((ymod(j), zmod(k + nz - 1), 1 - x)))
 
     z_range(0, wave_three)
-    y_range(lambda j: absorb(ymod(j), zmod(nz - 1), 1 - x))
+    y_range(lambda j: absorb((ymod(j), zmod(nz - 1), 1 - x)))
 
     total = acc_c[:, 0:1]
-    y_out[...] = (acc[...] / total).astype(jnp.bfloat16)
-    c_out[...] = acc_c[...] / total
-
+    own_c[...] = (acc_c[...] / total).reshape(rows, cols, 128)
+    own_y[...] = (acc[...] / total).reshape(rows, cols, width).astype(jnp.bfloat16)
+    for item in late:
+        item.start()
+    for item in halos:
+        item.wait_recv()
+    x_out[...] = widen(f1, x_bufs)
+    ext_c[...] = jnp.zeros_like(ext_c)
+    ext_c[2 : rows + 2, 0:cols] = own_c[...]
+    for item in late:
+        item.wait_recv()
+    ext_c[1:2, 0:cols] = c_bufs[0][...]
+    ext_c[rows + 2 : rows + 3, 0:cols] = c_bufs[1][...]
+    spot_c = lax.broadcasted_iota(jnp.int32, (rows, SIDE, 128), 1)
+    ext_c[2 : rows + 2, cols : cols + SIDE] = jnp.where(
+        spot_c < SIDE // 2, c_bufs[3][...], c_bufs[2][...]
+    )
+    c_out[...] = ext_c[...].reshape(count, 128)
+    y_out[...] = widen(own_y, y_bufs)
+
+    for item in late:
+        item.wait_send()
     for item in halos:
         item.wait_send()
     for k in range(1, nz):
@@ -374,6 +419,12 @@
     vmem = pl.BlockSpec(memory_space=pltpu.VMEM)
     dma = pltpu.SemaphoreType.DMA
     bf = jnp.bfloat16
+    edges = (
+        pltpu.VMEM((2, cols, width), bf),
+        pltpu.VMEM((2, cols, width), bf),
+        pltpu.VMEM((rows + 4, 16, width), bf),
+        pltpu.VMEM((rows + 4, 16, width), bf),
+    )
     xq, warped, sums = pl.pallas_call(
         functools.partial(gather_attend, nblk, ncol),
         out_shape=(
@@ -385,21 +436,29 @@
         out_specs=(vmem, vmem, vmem),
         scratch_shapes=[
             pltpu.VMEM((ncol, nblk, rows, cols, width), bf),
-            pltpu.VMEM((2, cols, width), bf),
-            pltpu.VMEM((2, cols, width), bf),
-            pltpu.VMEM((rows + 4, 16, width), bf),
-            pltpu.VMEM((rows + 4, 16, width), bf),
+            edges,
+            edges,
+            (
+                pltpu.VMEM((1, cols, 128), jnp.float32),
+                pltpu.VMEM((1, cols, 128), jnp.float32),
+                pltpu.VMEM((rows, SIDE, 128), jnp.float32),
+                pltpu.VMEM((rows, SIDE, 128), jnp.float32),
+            ),
+            pltpu.VMEM((rows, cols, width), bf),
+            pltpu.VMEM((rows, cols, 128), jnp.float32),
+            pltpu.VMEM((rows * cols, width), bf),
             pltpu.VMEM((rows + 4, cols + SIDE, width), jnp.float32),
-            pltpu.VMEM((count, 128), jnp.float32),
-            pltpu.VMEM((count, width), jnp.float32),
-            pltpu.VMEM((count, 128), jnp.float32),
+            pltpu.VMEM((rows + 4, cols + SIDE, 128), jnp.float32),
+            pltpu.VMEM((rows * cols, 128), jnp.float32),
+            pltpu.VMEM((rows * cols, width), jnp.float32),
+            pltpu.VMEM((rows * cols, 128), jnp.float32),
             dma((ncol, nblk, 2)),
             dma((nz - 1, 2)),
             dma((2, ncol, nz)),
             dma((2, ncol - 1, nz, 2)),
             dma((ncol, nblk // 2, 2)),
-            dma((8,)),
-            dma((8,)),
+            dma((20,)),
+            dma((20,)),
         ],
         compiler_params=pltpu.CompilerParams(
             collective_id=0, has_side_effects=True, vmem_limit_bytes=48 * 1024 * 1024

time: 46.3 us -> 44.7 us (0.965)
  Pallas kernels: 43.7 us -> 42.1 us
    pallas_call x1, Pallas kernels: 41 us -> 39.4 us  [body(): pl.pallas_call(functools.partial(gather_attend, nblk, ncol), out_shape=(j...]
where the time goes in v2:
time: 44.7 us; the launch traced here: 44.5 us
  Pallas kernels  42.1 us (94%)
  local copies, waits for them, and re-layouts  1.78 us (4%)
  between operations  0.65 us (1%)
    pallas_call x1, Pallas kernels, body(): pl.pallas_call(functools.partial(gather_attend, nblk, ncol), out_shape=(j...  39.4 us
    pallas_call x1, Pallas kernels, body(): pl.pallas_call(functools.partial(stencil, nblk, ncol, rows, cols), out_sh...  2.67 us
    unnamed x4, local copies, waits for them, and re-layouts  1.78 us

profile of v2, /device:TPU:0, one launch (start us, length us, event | category | flops | bytes accessed | tf_op | source)
XLA Modules:
  0.0 44.5 jit_solution(5166687802765234567)
XLA Ops:
  0.6 0.0 copy-start
  0.6 0.9 %copy-done = bf16[4,48,256]{2,1,0:T(8,128)(2,1)S(1)} copy-done((bf16[4,48,256]{2,1,0:T(8,128)(2,1)S(1)}, bf16[4,48,256]{2,1,0:T(8,128)(2,1)}, u32[]{:S(2)}) %copy-start) | copy-done | bytes 98328
  1.5 0.0 copy-start.1
  1.5 0.9 %copy-done.1 = bf16[4,48,256]{2,1,0:T(8,128)(2,1)S(1)} copy-done((bf16[4,48,256]{2,1,0:T(8,128)(2,1)S(1)}, bf16[4,48,256]{2,1,0:T(8,128)(2,1)}, u32[]{:S(2)}) %copy-start.1) | copy-done | bytes 98328
  2.4 39.4 %shard_map.49 = (bf16[448,256]{1,0:T(8,128)(2,1)S(1)}, bf16[448,256]{1,0:T(8,128)(2,1)S(1)}, f32[448,128]{1,0:T(8,128)S(1)}) custom-call(bf16[4,48,256]{2,1,0:T(8,128)(2,1)S(1)} %copy-done, bf16[4,48,256]{2,1,0:T(8,128)(2,1)S(1)} %copy-done.1), custom_call_target="tpu_custom_call" | custom-call | tf_op jit(solution)/shard_map/pallas_call | solution.py:428
  41.9 2.7 %shard_map.50 = (f32[2,4,48]{2,1,0:T(4,128)}, f32[2,4,48]{2,1,0:T(4,128)}, f32[4,48,256]{2,1,0:T(8,128)}) custom-call(bf16[448,256]{1,0:T(8,128)(2,1)S(1)} %get-tuple-element.6.x_ref, bf16[448,256]{1,0:T(8,128)(2,1)S(1)} %get-tuple-element.7.y_ref, f32[448,128]{1,0:T(8,128)S(1)} %get-tuple-element.8.c_ref), custom_call_target="tpu_custom_call" | custom-call | tf_op jit(solution)/shard_map/pallas_call | solution.py:467
Async XLA Ops:
  0.6 0.9 %copy-start = (bf16[4,48,256]{2,1,0:T(8,128)(2,1)S(1)}, bf16[4,48,256]{2,1,0:T(8,128)(2,1)}, u32[]{:S(2)}) copy-start(bf16[4,48,256]{2,1,0:T(8,128)(2,1)} %f1.1) | copy-start | bytes 294916
  1.5 0.9 %copy-start.1 = (bf16[4,48,256]{2,1,0:T(8,128)(2,1)S(1)}, bf16[4,48,256]{2,1,0:T(8,128)(2,1)}, u32[]{:S(2)}) copy-start(bf16[4,48,256]{2,1,0:T(8,128)(2,1)} %f2.1) | copy-start | bytes 294916

commit v3 on v2

--- a/solution.py
+++ b/solution.py
@@ -33,7 +33,13 @@
         return (zz * 2 + xx) * 2 + cc
 
     def zmod(k):
-        return lax.rem(z + k, nz)
+        if nz & (nz - 1):
+            return lax.rem(z + k, nz)
+        found = 0
+        for bit in range(nz.bit_length() - 1):
+            step = 2**bit
+            found = found + lax.rem(z // step + k // step, 2) * step
+        return found
 
     def ymod(k):
         return lax.rem(y + k, ncol)
@@ -242,7 +248,7 @@
 
         @pl.when(k > 0)
         def _():
-            absorb_two(zmod(k + nz - 1))
+            absorb_two(zmod(k - 1))
 
     z_range(0, wave_two)
 
@@ -264,7 +270,7 @@
 
         @pl.when(k > 0)
         def _():
-            y_range(lambda j: absorb((ymod(j), zmod(k + nz - 1), 1 - x)))
+            y_range(lambda j: absorb((ymod(j), zmod(k - 1), 1 - x)))
 
     z_range(0, wave_three)
     y_range(lambda j: absorb((ymod(j), zmod(nz - 1), 1 - x)))

time: 44.7 us -> 42.9 us (0.960)
  Pallas kernels: 42.1 us -> 40.3 us
    pallas_call x1, Pallas kernels: 39.4 us -> 37.7 us  [body(): pl.pallas_call(functools.partial(gather_attend, nblk, ncol), out_shape=(j...]
where the time goes in v3:
time: 42.9 us; the launch traced here: 42.8 us
  Pallas kernels  40.3 us (94%)
  local copies, waits for them, and re-layouts  1.78 us (4%)
  between operations  0.65 us (2%)
    pallas_call x1, Pallas kernels, body(): pl.pallas_call(functools.partial(gather_attend, nblk, ncol), out_shape=(j...  37.7 us
    pallas_call x1, Pallas kernels, body(): pl.pallas_call(functools.partial(stencil, nblk, ncol, rows, cols), out_sh...  2.67 us
    unnamed x4, local copies, waits for them, and re-layouts  1.78 us

profile of v3, /device:TPU:0, one launch (start us, length us, event | category | flops | bytes accessed | tf_op | source)
XLA Modules:
  0.0 42.8 jit_solution(12494797966174009423)
XLA Ops:
  0.6 0.0 copy-start
  0.6 0.9 %copy-done = bf16[4,48,256]{2,1,0:T(8,128)(2,1)S(1)} copy-done((bf16[4,48,256]{2,1,0:T(8,128)(2,1)S(1)}, bf16[4,48,256]{2,1,0:T(8,128)(2,1)}, u32[]{:S(2)}) %copy-start) | copy-done | bytes 98328
  1.5 0.0 copy-start.1
  1.5 0.9 %copy-done.1 = bf16[4,48,256]{2,1,0:T(8,128)(2,1)S(1)} copy-done((bf16[4,48,256]{2,1,0:T(8,128)(2,1)S(1)}, bf16[4,48,256]{2,1,0:T(8,128)(2,1)}, u32[]{:S(2)}) %copy-start.1) | copy-done | bytes 98328
  2.4 37.7 %shard_map.49 = (bf16[448,256]{1,0:T(8,128)(2,1)S(1)}, bf16[448,256]{1,0:T(8,128)(2,1)S(1)}, f32[448,128]{1,0:T(8,128)S(1)}) custom-call(bf16[4,48,256]{2,1,0:T(8,128)(2,1)S(1)} %copy-done, bf16[4,48,256]{2,1,0:T(8,128)(2,1)S(1)} %copy-done.1), custom_call_target="tpu_custom_call" | custom-call | tf_op jit(solution)/shard_map/pallas_call | solution.py:434
  40.1 2.7 %shard_map.50 = (f32[2,4,48]{2,1,0:T(4,128)}, f32[2,4,48]{2,1,0:T(4,128)}, f32[4,48,256]{2,1,0:T(8,128)}) custom-call(bf16[448,256]{1,0:T(8,128)(2,1)S(1)} %get-tuple-element.6.x_ref, bf16[448,256]{1,0:T(8,128)(2,1)S(1)} %get-tuple-element.7.y_ref, f32[448,128]{1,0:T(8,128)S(1)} %get-tuple-element.8.c_ref), custom_call_target="tpu_custom_call" | custom-call | tf_op jit(solution)/shard_map/pallas_call | solution.py:473
Async XLA Ops:
  0.6 0.9 %copy-start = (bf16[4,48,256]{2,1,0:T(8,128)(2,1)S(1)}, bf16[4,48,256]{2,1,0:T(8,128)(2,1)}, u32[]{:S(2)}) copy-start(bf16[4,48,256]{2,1,0:T(8,128)(2,1)} %f1.1) | copy-start | bytes 294916
  1.5 0.9 %copy-start.1 = (bf16[4,48,256]{2,1,0:T(8,128)(2,1)S(1)}, bf16[4,48,256]{2,1,0:T(8,128)(2,1)}, u32[]{:S(2)}) copy-start(bf16[4,48,256]{2,1,0:T(8,128)(2,1)} %f2.1) | copy-start | bytes 294916

commit v4 on v3

--- a/solution.py
+++ b/solution.py
@@ -228,10 +228,6 @@
 
         y_range(take)
 
-        @pl.when(k > 0)
-        def _():
-            absorb((y, zz, x))
-
     z_range(0, wave_one)
 
     def wave_two(k):
@@ -248,6 +244,7 @@
 
         @pl.when(k > 0)
         def _():
+            absorb((y, zz, x))
             absorb_two(zmod(k - 1))
 
     z_range(0, wave_two)

time: 42.9 us -> 43.7 us (1.019)
  Pallas kernels: 40.3 us -> 41.1 us
    pallas_call x1, Pallas kernels: 37.7 us -> 38.5 us  [body(): pl.pallas_call(functools.partial(gather_attend, nblk, ncol), out_shape=(j...]
where the time goes in v4:
time: 43.7 us; the launch traced here: 43.6 us
  Pallas kernels  41.1 us (94%)
  local copies, waits for them, and re-layouts  1.78 us (4%)
  between operations  0.65 us (1%)
    pallas_call x1, Pallas kernels, body(): pl.pallas_call(functools.partial(gather_attend, nblk, ncol), out_shape=(j...  38.5 us
    pallas_call x1, Pallas kernels, body(): pl.pallas_call(functools.partial(stencil, nblk, ncol, rows, cols), out_sh...  2.67 us
    unnamed x4, local copies, waits for them, and re-layouts  1.78 us

profile of v4, /device:TPU:0, one launch (start us, length us, event | category | flops | bytes accessed | tf_op | source)
XLA Modules:
  0.0 43.6 jit_solution(4390737860681348805)
XLA Ops:
  0.6 0.0 copy-start
  0.6 0.9 %copy-done = bf16[4,48,256]{2,1,0:T(8,128)(2,1)S(1)} copy-done((bf16[4,48,256]{2,1,0:T(8,128)(2,1)S(1)}, bf16[4,48,256]{2,1,0:T(8,128)(2,1)}, u32[]{:S(2)}) %copy-start) | copy-done | bytes 98328
  1.5 0.0 copy-start.1
  1.5 0.9 %copy-done.1 = bf16[4,48,256]{2,1,0:T(8,128)(2,1)S(1)} copy-done((bf16[4,48,256]{2,1,0:T(8,128)(2,1)S(1)}, bf16[4,48,256]{2,1,0:T(8,128)(2,1)}, u32[]{:S(2)}) %copy-start.1) | copy-done | bytes 98328
  2.4 38.5 %shard_map.49 = (bf16[448,256]{1,0:T(8,128)(2,1)S(1)}, bf16[448,256]{1,0:T(8,128)(2,1)S(1)}, f32[448,128]{1,0:T(8,128)S(1)}) custom-call(bf16[4,48,256]{2,1,0:T(8,128)(2,1)S(1)} %copy-done, bf16[4,48,256]{2,1,0:T(8,128)(2,1)S(1)} %copy-done.1), custom_call_target="tpu_custom_call" | custom-call | tf_op jit(solution)/shard_map/pallas_call | solution.py:431
  40.9 2.7 %shard_map.50 = (f32[2,4,48]{2,1,0:T(4,128)}, f32[2,4,48]{2,1,0:T(4,128)}, f32[4,48,256]{2,1,0:T(8,128)}) custom-call(bf16[448,256]{1,0:T(8,128)(2,1)S(1)} %get-tuple-element.6.x_ref, bf16[448,256]{1,0:T(8,128)(2,1)S(1)} %get-tuple-element.7.y_ref, f32[448,128]{1,0:T(8,128)S(1)} %get-tuple-element.8.c_ref), custom_call_target="tpu_custom_call" | custom-call | tf_op jit(solution)/shard_map/pallas_call | solution.py:470
Async XLA Ops:
  0.6 0.9 %copy-start = (bf16[4,48,256]{2,1,0:T(8,128)(2,1)S(1)}, bf16[4,48,256]{2,1,0:T(8,128)(2,1)}, u32[]{:S(2)}) copy-start(bf16[4,48,256]{2,1,0:T(8,128)(2,1)} %f1.1) | copy-start | bytes 294916
  1.5 0.9 %copy-start.1 = (bf16[4,48,256]{2,1,0:T(8,128)(2,1)S(1)}, bf16[4,48,256]{2,1,0:T(8,128)(2,1)}, u32[]{:S(2)}) copy-start(bf16[4,48,256]{2,1,0:T(8,128)(2,1)} %f2.1) | copy-start | bytes 294916

commit v5 on v3

--- a/solution.py
+++ b/solution.py
@@ -132,8 +132,6 @@
     for k in range(1, nz):
         z_copy(k, 0).start()
         z_copy(k, 1).start()
-    for item in halos:
-        item.start()
     start_column(z)
 
     peak[...] = jnp.full_like(peak, -1e30)
@@ -213,6 +211,8 @@
         start_column(zz)
 
     z_range(1, wave_z)
+    for item in halos:
+        item.start()
 
     def wave_one(k):
         zz = zmod(k)

time: 42.9 us -> 42.9 us (level)
  no operation moved by 1% of the time
where the time goes in v5:
time: 42.9 us; the launch traced here: 42.7 us
  Pallas kernels  40.3 us (94%)
  local copies, waits for them, and re-layouts  1.78 us (4%)
  between operations  0.65 us (2%)
    pallas_call x1, Pallas kernels, body(): pl.pallas_call(functools.partial(gather_attend, nblk, ncol), out_shape=(j...  37.6 us
    pallas_call x1, Pallas kernels, body(): pl.pallas_call(functools.partial(stencil, nblk, ncol, rows, cols), out_sh...  2.67 us
    unnamed x4, local copies, waits for them, and re-layouts  1.78 us

profile of v5, /device:TPU:0, one launch (start us, length us, event | category | flops | bytes accessed | tf_op | source)
XLA Modules:
  0.0 42.7 jit_solution(10312418928533072417)
XLA Ops:
  0.6 0.0 copy-start
  0.6 0.9 %copy-done = bf16[4,48,256]{2,1,0:T(8,128)(2,1)S(1)} copy-done((bf16[4,48,256]{2,1,0:T(8,128)(2,1)S(1)}, bf16[4,48,256]{2,1,0:T(8,128)(2,1)}, u32[]{:S(2)}) %copy-start) | copy-done | bytes 98328
  1.5 0.0 copy-start.1
  1.5 0.9 %copy-done.1 = bf16[4,48,256]{2,1,0:T(8,128)(2,1)S(1)} copy-done((bf16[4,48,256]{2,1,0:T(8,128)(2,1)S(1)}, bf16[4,48,256]{2,1,0:T(8,128)(2,1)}, u32[]{:S(2)}) %copy-start.1) | copy-done | bytes 98328
  2.4 37.6 %shard_map.49 = (bf16[448,256]{1,0:T(8,128)(2,1)S(1)}, bf16[448,256]{1,0:T(8,128)(2,1)S(1)}, f32[448,128]{1,0:T(8,128)S(1)}) custom-call(bf16[4,48,256]{2,1,0:T(8,128)(2,1)S(1)} %copy-done, bf16[4,48,256]{2,1,0:T(8,128)(2,1)S(1)} %copy-done.1), custom_call_target="tpu_custom_call" | custom-call | tf_op jit(solution)/shard_map/pallas_call | solution.py:434
  40.1 2.7 %shard_map.50 = (f32[2,4,48]{2,1,0:T(4,128)}, f32[2,4,48]{2,1,0:T(4,128)}, f32[4,48,256]{2,1,0:T(8,128)}) custom-call(bf16[448,256]{1,0:T(8,128)(2,1)S(1)} %get-tuple-element.6.x_ref, bf16[448,256]{1,0:T(8,128)(2,1)S(1)} %get-tuple-element.7.y_ref, f32[448,128]{1,0:T(8,128)S(1)} %get-tuple-element.8.c_ref), custom_call_target="tpu_custom_call" | custom-call | tf_op jit(solution)/shard_map/pallas_call | solution.py:473
Async XLA Ops:
  0.6 0.9 %copy-start = (bf16[4,48,256]{2,1,0:T(8,128)(2,1)S(1)}, bf16[4,48,256]{2,1,0:T(8,128)(2,1)}, u32[]{:S(2)}) copy-start(bf16[4,48,256]{2,1,0:T(8,128)(2,1)} %f1.1) | copy-start | bytes 294916
  1.5 0.9 %copy-start.1 = (bf16[4,48,256]{2,1,0:T(8,128)(2,1)S(1)}, bf16[4,48,256]{2,1,0:T(8,128)(2,1)}, u32[]{:S(2)}) copy-start(bf16[4,48,256]{2,1,0:T(8,128)(2,1)} %f2.1) | copy-start | bytes 294916
